TPU v7x, 32 devices: a whole 2x2x4 slice. The times are simulated.
32 devices in a mesh: groups: 2 (over x), samples: 16 (over z, y, core).
Axes of the slice: x: 2, y: 2, z: 4, core: 2. Of those that a mesh axis runs over, the one named last changes fastest.
Arguments:
- energies: float32 [256, 393216], P(None, ('groups', 'samples')), parts along dimension 1, may hold values from -700 to 700
- mult: int32 [393216, 256], P(('groups', 'samples')), parts along dimension 0, may hold values from 0 to 3
- state_counts: int32 [512], P('groups'), parts along dimension 0, may hold values from 1 to 1536, 196608 in all
Outputs:
- free_energy: float32 [512, 256], P('groups'), parts along dimension 0
There are 2 independent parts, one for each index of `groups`. A program takes and returns all parts, laid end to end along the dimension named above; each array names one. Nothing has to cross between parts.
All inputs are finite; a program needn't handle non-finite values.
Results may differ from a plain program's by a relative error of at most 0.0003.
Values sent between devices are 32-bit elements; how exact they have to be, the bound alone decides.
A program may use at most 128 MiB of HBM per device.

v0:
```python
import jax
import jax.numpy as jnp
from jax import lax
from jax.sharding import PartitionSpec as P

ITERS = 4


def weighted_terms(boltz, weight, mult_part):
    denom = lax.dot_general(
        boltz, weight, (((0,), (0,)), ((), ())), preferred_element_type=jnp.float32
    )
    ratio = (mult_part.astype(jnp.float32) / denom).astype(jnp.bfloat16)
    return jnp.dot(boltz, ratio, preferred_element_type=jnp.float32)


def settle(partial_sums):
    totals = lax.psum(partial_sums, "samples")
    logs = jnp.log(totals)
    return logs[0:1] - logs


def on_device(energies, mult, state_counts):
    shift = jnp.min(energies, axis=0, keepdims=True)
    boltz = jnp.exp(shift - energies).astype(jnp.bfloat16)
    counts_f = state_counts.astype(jnp.float32)[:, None]
    num_states = energies.shape[0]
    num_reps = mult.shape[1]
    free = jnp.zeros((num_states, num_reps), jnp.float32)
    for step in range(ITERS):
        weight = (counts_f * jnp.exp(free)).astype(jnp.bfloat16)
        free = settle(weighted_terms(boltz, weight, mult))
    return free


def solution(mesh):
    in_specs = (P(None, ("groups", "samples")), P(("groups", "samples"), None), P("groups"))
    out_specs = P("groups", None)
    return jax.shard_map(
        on_device, mesh=mesh, in_specs=in_specs, out_specs=out_specs, check_vma=False
    )
```

profile of v0, /device:TPU:0, one launch (start us, length us, event | category | flops | bytes accessed | tf_op | source)
XLA Modules:
  0.0 444.1 jit_solution(2489789016998661210)
XLA Ops:
  6.5 0.0 all-reduce.5.cloned.1.call-start
  6.5 0.7 fusion.24
  7.2 5.2 %reduce_min.9 = f32[12288]{0:T(1024)S(1)} reduce(f32[256,12288]{1,0:T(8,128)} %param.3, f32[]{:T(128)} %constant.0.clone.1), dimensions={0}, to_apply=%region_0.0 | reduce | flops 3133440 | bytes 12632068 | tf_op jit(solution)/shard_map/reduce_min | solution.py:24
  12.4 9.0 %exponential_convert_fusion = bf16[256,12288]{1,0:T(8,128)(2,1)} fusion(f32[256,12288]{1,0:T(8,128)} %param.3, f32[12288]{0:T(1024)S(1)} %reduce_min.9), kind=kLoop, calls=%fused_computation.4 | loop fusion | flops 6291456 | bytes 18923520 | tf_op jit(solution)/shard_map/convert_element_type | solution.py:25
  21.4 12.6 %fusion = f32[256,256]{1,0:T(8,128)} fusion(bf16[256,12288]{1,0:T(8,128)(2,1)} %exponential_convert_fusion, s32[12288,256]{1,0:T(8,128)} %param.4, bf16[256]{0:T(256)(128)(2,1)S(1)} %get-tuple-element.6), kind=kOutput, calls=%fused_computation.5 | convolution fusion | flops 3230662656 | bytes 19137024 | tf_op jit(solution)/shard_map/dot_general | solution.py:14
  34.0 0.0 all-reduce.5.cloned.1.call-update
  34.0 0.0 all-reduce.7.cloned.1.call-start
  34.0 91.5 %all-reduce.5.cloned.1.call-done = f32[256,256]{1,0:T(8,128)} async-done(((f32[256,256]{1,0:T(8,128)}), f32[256,256]{1,0:T(8,128)}) %all-reduce.5.cloned.1.call-update) | async-done | bytes 262160 | tf_op jit(solution)/shard_map/psum | solution.py:18
  125.5 1.0 log.12
  126.5 12.7 %fusion.1 = f32[256,256]{1,0:T(8,128)} fusion(bf16[256,12288]{1,0:T(8,128)(2,1)} %exponential_convert_fusion, s32[12288,256]{1,0:T(8,128)} %param.4, f32[256]{0:T(256)S(1)} %bitcast.14, f32[256]{0:T(256)S(1)} %get-tuple-element.5, f32[256,256]{1,0:T(8,128)} %all-reduce.5.cloned.1.call-done), kind=kOutput, calls=%fused_computation.6 | convolution fusion | flops 3230859264 | bytes 19400704 | tf_op jit(solution)/shard_map/dot_general | solution.py:14
  139.2 0.0 all-reduce.7.cloned.1.call-update
  139.2 0.2 all-reduce.9.cloned.1.call-start
  139.4 89.2 %all-reduce.7.cloned.1.call-done = f32[256,256]{1,0:T(8,128)} async-done(((f32[256,256]{1,0:T(8,128)}), f32[256,256]{1,0:T(8,128)}) %all-reduce.7.cloned.1.call-update) | async-done | bytes 262160 | tf_op jit(solution)/shard_map/psum | solution.py:18
  228.6 1.0 log.13
  229.6 12.7 %fusion.2 = f32[256,256]{1,0:T(8,128)} fusion(bf16[256,12288]{1,0:T(8,128)(2,1)} %exponential_convert_fusion, s32[12288,256]{1,0:T(8,128)} %param.4, f32[256]{0:T(256)S(1)} %bitcast.15, f32[256]{0:T(256)S(1)} %get-tuple-element.5, f32[256,256]{1,0:T(8,128)} %all-reduce.7.cloned.1.call-done), kind=kOutput, calls=%fused_computation.7 | convolution fusion | flops 3230859264 | bytes 19400704 | tf_op jit(solution)/shard_map/dot_general | solution.py:14
  242.3 0.0 all-reduce.9.cloned.1.call-update
  242.3 0.0 all-reduce.11.cloned.1.call-start
  242.4 89.4 %all-reduce.9.cloned.1.call-done = f32[256,256]{1,0:T(8,128)} async-done(((f32[256,256]{1,0:T(8,128)}), f32[256,256]{1,0:T(8,128)}) %all-reduce.9.cloned.1.call-update) | async-done | bytes 262160 | tf_op jit(solution)/shard_map/psum | solution.py:18
  331.8 1.0 log.14
  332.8 12.7 %fusion.3 = f32[256,256]{1,0:T(8,128)} fusion(bf16[256,12288]{1,0:T(8,128)(2,1)} %exponential_convert_fusion, s32[12288,256]{1,0:T(8,128)} %param.4, f32[256]{0:T(256)S(1)} %bitcast.13, f32[256]{0:T(256)S(1)} %get-tuple-element.5, f32[256,256]{1,0:T(8,128)} %all-reduce.9.cloned.1.call-done), kind=kOutput, calls=%fused_computation.8 | convolution fusion | flops 3230859264 | bytes 19400704 | tf_op jit(solution)/shard_map/dot_general | solution.py:14
  345.4 0.0 all-reduce.11.cloned.1.call-update
  345.4 89.4 %all-reduce.11.cloned.1.call-done = f32[256,256]{1,0:T(8,128)} async-done(((f32[256,256]{1,0:T(8,128)}), f32[256,256]{1,0:T(8,128)}) %all-reduce.11.cloned.1.call-update) | async-done | bytes 262160 | tf_op jit(solution)/shard_map/psum | solution.py:18
  434.9 1.0 log.15
  435.9 1.7 broadcast_subtract_fusion
  (4 shorter events, 0.0 us)
Async XLA Ops:
  6.5 119.0 %all-reduce.5.cloned.1.call-start = ((), (), s32[]{:S(2)}) async-start(), calls=%async_computation | async-start | bytes 524288 | tf_op jit(solution)/shard_map/psum | solution.py:18
  34.0 194.7 %all-reduce.7.cloned.1.call-start = ((), (), s32[]{:S(2)}) async-start(), calls=%async_computation.1 | async-start | bytes 524288 | tf_op jit(solution)/shard_map/psum | solution.py:18
  139.2 192.5 %all-reduce.9.cloned.1.call-start = ((), (), s32[]{:S(2)}) async-start(), calls=%async_computation.2 | async-start | bytes 524288 | tf_op jit(solution)/shard_map/psum | solution.py:18
  242.3 192.5 %all-reduce.11.cloned.1.call-start = ((), (), s32[]{:S(2)}) async-start(), calls=%async_computation.3 | async-start | bytes 524288 | tf_op jit(solution)/shard_map/psum | solution.py:18
Sparse Core Ops, SparseCore 0:
  34.1 91.3 all-reduce.4
  139.3 89.2 all-reduce.6
  242.5 89.2 all-reduce.8
  345.6 89.2 all-reduce.10
where the time goes:
time: 445 us; the launch traced here: 444 us
  waiting for transfers between devices  360 us (81%)
  matrix products  50.6 us (11%)
  other arithmetic  16.5 us (4%)
  between operations  13.2 us (3%)
    psum x4, waiting for transfers between devices, settle(): totals = lax.psum(partial_sums, 'samples')  360 us
    dot_general x4, matrix products, weighted_terms(): return jnp.dot(boltz, ratio, preferred_element_type=jnp.float32)  50.6 us
    convert_element_type x1, other arithmetic, on_device(): boltz = jnp.exp(shift - energies).astype(jnp.bfloat16)  8.95 us
  transfers between devices with their start and end apart: 4, of which 4 were waited for; matrix products, arithmetic and copies ran while one was open for 0% of the time, Pallas kernels for 0%

commit v1 on v0

v1 whole, which is shorter than its diff:
```python
import functools

import jax
import jax.numpy as jnp
from jax import lax
from jax.experimental import pallas as pl
from jax.experimental.pallas import tpu as pltpu
from jax.sharding import PartitionSpec as P

ITERS = 4
CHUNK = 1024


def mbar_kernel(num_dev, counts_ref, e_hbm, m_hbm, out_ref, e_buf, m_buf, bz, bzt, weight,
                counts, acc, half, core_recv, part_recv, gathered,
                e_sem, m_sem, core_sem, part_send, part_sem, gat_send, gat_sem, fwd_send, fwd_sem):
    states, reps = acc.shape
    samples = e_buf.shape[1]
    chunks = samples // CHUNK
    chips = num_dev // 2
    hrows = states // 2
    prows = hrows // chips
    me = lax.axis_index("samples")
    chip, core = me // 2, lax.rem(me, 2)
    other = 1 - core

    def device(chip_at, core_at):
        return {"samples": chip_at * 2 + core_at}

    def chip_ahead(d):
        return lax.rem(chip + d, chips)

    def chip_behind(d):
        return lax.rem(chip + (chips - d), chips)

    def e_copy(i):
        cols = pl.ds(pl.multiple_of(i * CHUNK, CHUNK), CHUNK)
        return pltpu.make_async_copy(e_hbm.at[:, cols], e_buf.at[:, cols], e_sem.at[i])

    def m_copy(i):
        rows = pl.ds(pl.multiple_of(i * CHUNK, CHUNK), CHUNK)
        return pltpu.make_async_copy(m_hbm.at[rows, :], m_buf.at[rows, :], m_sem.at[i])

    @pl.loop(0, chunks)
    def _(i):
        e_copy(i).start()
        m_copy(i).start()

    barrier = pltpu.get_barrier_semaphore()
    pl.semaphore_signal(barrier, inc=1, device_id=device(chip, other))
    for d in range(1, chips):
        pl.semaphore_signal(barrier, inc=1, device_id=device(chip_ahead(d), core))

    counts[...] = jnp.broadcast_to(counts_ref[...].astype(jnp.float32), (reps, states)).T
    weight[...] = counts[...].astype(jnp.bfloat16)

    def terms(i, boltz, boltz_t):
        rows = pl.ds(pl.multiple_of(i * CHUNK, CHUNK), CHUNK)
        denom = jnp.dot(boltz_t, weight[...], preferred_element_type=jnp.float32)
        ratio = (m_buf[rows, :].astype(jnp.float32) / denom).astype(jnp.bfloat16)
        acc[...] += jnp.dot(boltz, ratio, preferred_element_type=jnp.float32)

    def all_reduce(t):
        def to_core(rows, sem):
            return pltpu.make_async_remote_copy(
                src_ref=acc.at[rows], dst_ref=core_recv.at[t],
                send_sem=core_sem.at[t, 0], recv_sem=core_sem.at[t, 1],
                device_id=device(chip, other))

        core_copy = to_core(pl.ds(pl.multiple_of(other * hrows, hrows), hrows), core_sem)
        core_copy.start()
        core_copy.wait_recv()

        def part_of(at):
            return pl.ds(pl.multiple_of(at * prows, prows), prows)

        def row_of(core_at, chip_at):
            return pl.ds(pl.multiple_of(core_at * hrows + chip_at * prows, prows), prows)

        sends = [core_copy]
        part_copies = []
        for d in range(1, chips):
            to = chip_ahead(d)
            half[t, part_of(to), :] = acc[row_of(core, to), :] + core_recv[t, part_of(to), :]
            copy = pltpu.make_async_remote_copy(
                src_ref=half.at[t, part_of(to)], dst_ref=part_recv.at[t, d - 1],
                send_sem=part_send.at[t, d - 1], recv_sem=part_sem.at[t, d - 1],
                device_id=device(to, core))
            copy.start()
            part_copies.append(copy)
        total = acc[row_of(core, chip), :] + core_recv[t, part_of(chip), :]
        for d in range(1, chips):
            part_copies[d - 1].wait_recv()
            total = total + part_recv[t, d - 1]
        mine = row_of(core, chip)
        gathered[t, mine, :] = total

        gat_copies = []
        for d in range(1, chips):
            copy = pltpu.make_async_remote_copy(
                src_ref=gathered.at[t, mine], dst_ref=gathered.at[t, mine],
                send_sem=gat_send.at[t, d - 1], recv_sem=gat_sem.at[t, d - 1],
                device_id=device(chip_ahead(d), core))
            copy.start()
            gat_copies.append(copy)
        fwd_copies = []
        for d in range(chips):
            if d > 0:
                gat_copies[d - 1].wait_recv()
            rows = row_of(core, chip_behind(d))
            copy = pltpu.make_async_remote_copy(
                src_ref=gathered.at[t, rows], dst_ref=gathered.at[t, rows],
                send_sem=fwd_send.at[t, d], recv_sem=fwd_sem.at[t, d],
                device_id=device(chip, other))
            copy.start()
            fwd_copies.append(copy)
        for copy in fwd_copies:
            copy.wait_recv()
        for copy in [core_copy] + part_copies + gat_copies + fwd_copies:
            copy.wait_send()

    acc[...] = jnp.zeros_like(acc)

    @pl.loop(0, chunks)
    def _(i):
        cols = pl.ds(pl.multiple_of(i * CHUNK, CHUNK), CHUNK)
        e_copy(i).wait()
        e = e_buf[:, cols]
        boltz = jnp.exp(jnp.min(e, axis=0, keepdims=True) - e).astype(jnp.bfloat16)
        bz[:, cols] = boltz
        boltz_t = boltz.T
        bzt[cols, :] = boltz_t
        m_copy(i).wait()
        terms(i, boltz, boltz_t)

    pl.semaphore_wait(barrier, chips)

    for t in range(ITERS):
        all_reduce(t)
        if t < ITERS - 1:
            weight[...] = (counts[...] * (gathered[t, 0:1, :] / gathered[t])).astype(jnp.bfloat16)
            acc[...] = jnp.zeros_like(acc)

            @pl.loop(0, chunks)
            def _(i):
                cols = pl.ds(pl.multiple_of(i * CHUNK, CHUNK), CHUNK)
                terms(i, bz[:, cols], bzt[cols, :])

    out_ref[...] = gathered[ITERS - 1]


def on_device(num_dev, energies, mult, state_counts):
    states, samples = energies.shape
    reps = mult.shape[1]
    chips = num_dev // 2
    chunks = samples // CHUNK
    hrows = states // 2
    f32, bf16 = jnp.float32, jnp.bfloat16
    dma = pltpu.SemaphoreType.DMA
    totals = pl.pallas_call(
        functools.partial(mbar_kernel, num_dev),
        out_shape=jax.ShapeDtypeStruct((states, reps), f32),
        in_specs=[
            pl.BlockSpec(memory_space=pltpu.VMEM),
            pl.BlockSpec(memory_space=pl.ANY),
            pl.BlockSpec(memory_space=pl.ANY),
        ],
        out_specs=pl.BlockSpec(memory_space=pltpu.VMEM),
        scratch_shapes=[
            pltpu.VMEM((states, samples), f32),
            pltpu.VMEM((samples, reps), jnp.int32),
            pltpu.VMEM((states, samples), bf16),
            pltpu.VMEM((samples, states), bf16),
            pltpu.VMEM((states, reps), bf16),
            pltpu.VMEM((states, reps), f32),
            pltpu.VMEM((states, reps), f32),
            pltpu.VMEM((ITERS, hrows, reps), f32),
            pltpu.VMEM((ITERS, hrows, reps), f32),
            pltpu.VMEM((ITERS, chips - 1, hrows // chips, reps), f32),
            pltpu.VMEM((ITERS, states, reps), f32),
            dma((chunks,)),
            dma((chunks,)),
            dma((ITERS, 2)),
            dma((ITERS, chips - 1)),
            dma((ITERS, chips - 1)),
            dma((ITERS, chips - 1)),
            dma((ITERS, chips - 1)),
            dma((ITERS, chips)),
            dma((ITERS, chips)),
        ],
        compiler_params=pltpu.CompilerParams(
            collective_id=0, has_side_effects=True, vmem_limit_bytes=56 * 1024 * 1024
        ),
        cost_estimate=pl.CostEstimate(
            flops=4 * ITERS * states * samples * reps,
            bytes_accessed=4 * samples * (states + reps),
            transcendentals=states * samples,
        ),
    )(state_counts.reshape(1, states), energies, mult)
    logs = jnp.log(totals)
    return logs[0:1] - logs


def solution(mesh):
    in_specs = (P(None, ("groups", "samples")), P(("groups", "samples"), None), P("groups"))
    out_specs = P("groups", None)
    return jax.shard_map(
        functools.partial(on_device, mesh.shape["samples"]),
        mesh=mesh, in_specs=in_specs, out_specs=out_specs, check_vma=False,
    )
```

time: 445 us -> 90.8 us (0.20)
  waiting for transfers between devices: 360 us -> 0 us
  Pallas kernels: 0 us -> 87.9 us
  matrix products: 50.6 us -> 0 us
  other arithmetic: 16.5 us -> 1.7 us
  between operations: 13.2 us -> 0.02 us
    psum x4 -> x0, waiting for transfers between devices: 360 us -> none  [settle(): totals = lax.psum(partial_sums, 'samples')]
    pallas_call x0 -> x1, Pallas kernels: none -> 87.9 us  [on_device(): pl.pallas_call(functools.partial(mbar_kernel, num_dev), out_shape=jax.Sha...]
    dot_general x4 -> x0, matrix products: 50.6 us -> none  [weighted_terms(): return jnp.dot(boltz, ratio, preferred_element_type=jnp.float32)]
    convert_element_type x2 -> x0, other arithmetic: 9.64 us -> none  [the longest x1 8.95 us: on_device(): boltz = jnp.exp(shift - energies).astype(jnp.bfloat16)]
    reduce_min x1 -> x0, other arithmetic: 5.2 us -> none  [on_device(): shift = jnp.min(energies, axis=0, keepdims=True)]
  transfers between devices with their start and end apart: 4 -> 0, of which waited for: 4 -> 0; matrix products, arithmetic and copies ran while one was open for 0% -> 0% of each run, Pallas kernels for 0% -> 0%
where the time goes in v1:
time: 90.8 us; the launch traced here: 90.6 us
  Pallas kernels  87.9 us (97%)
  other arithmetic  1.7 us (2%)
  local copies, waits for them, and re-layouts  0.99 us (1%)
    pallas_call x1, Pallas kernels, on_device(): pl.pallas_call(functools.partial(mbar_kernel, num_dev), out_shape=jax.Sha...  87.9 us

profile of v1, /device:TPU:0, one launch (start us, length us, event | category | flops | bytes accessed | tf_op | source)
XLA Modules:
  0.0 90.6 jit_solution(17000931798051937065)
XLA Ops:
  0.0 87.9 %shard_map.37 = f32[256,256]{1,0:T(8,128)} custom-call(s32[1,256]{1,0:T(1,128)} %bitcast.3, f32[256,12288]{1,0:T(8,128)} %e_hbm.1, s32[12288,256]{1,0:T(8,128)} %m_hbm.1), custom_call_target="tpu_custom_call" | custom-call | flops 12884901888 | bytes 25165824 | tf_op jit(solution)/shard_map/pallas_call | solution.py:160
  87.9 1.0 %log.3 = f32[256,256]{1,0:T(8,128)S(1)} log(f32[256,256]{1,0:T(8,128)} %shard_map.37) | non-fusion elementwise | bytes 524288 | tf_op jit(solution)/shard_map/log | solution.py:200
  88.9 1.7 %broadcast_subtract_fusion = f32[256,256]{1,0:T(8,128)} fusion(f32[256]{0:T(256)S(1)} %bitcast.2, f32[256,256]{1,0:T(8,128)} %shard_map.37), kind=kLoop, calls=%fused_computation | loop fusion | flops 65536 | bytes 525312 | tf_op jit(solution)/shard_map/sub | solution.py:201
  (1 shorter events, 0.0 us)

commit v2 on v1

--- a/solution.py
+++ b/solution.py
@@ -8,12 +8,13 @@
 from jax.sharding import PartitionSpec as P
 
 ITERS = 4
-CHUNK = 1024
+CHUNK = 2048
+BIG = 6144
 
 
 def mbar_kernel(num_dev, counts_ref, e_hbm, m_hbm, out_ref, e_buf, m_buf, bz, bzt, weight,
                 counts, acc, half, core_recv, part_recv, gathered,
-                e_sem, m_sem, core_sem, part_send, part_sem, gat_send, gat_sem, fwd_send, fwd_sem):
+                e_sem, m_sem, core_send, core_sem, part_send, part_sem, gat_send, gat_sem, fwd_send, fwd_sem):
     states, reps = acc.shape
     samples = e_buf.shape[1]
     chunks = samples // CHUNK
@@ -27,11 +28,8 @@
     def device(chip_at, core_at):
         return {"samples": chip_at * 2 + core_at}
 
-    def chip_ahead(d):
-        return lax.rem(chip + d, chips)
-
-    def chip_behind(d):
-        return lax.rem(chip + (chips - d), chips)
+    def partner(d):
+        return lax.bitwise_xor(chip, d)
 
     def e_copy(i):
         cols = pl.ds(pl.multiple_of(i * CHUNK, CHUNK), CHUNK)
@@ -49,65 +47,66 @@
     barrier = pltpu.get_barrier_semaphore()
     pl.semaphore_signal(barrier, inc=1, device_id=device(chip, other))
     for d in range(1, chips):
-        pl.semaphore_signal(barrier, inc=1, device_id=device(chip_ahead(d), core))
+        pl.semaphore_signal(barrier, inc=1, device_id=device(partner(d), core))
 
     counts[...] = jnp.broadcast_to(counts_ref[...].astype(jnp.float32), (reps, states)).T
     weight[...] = counts[...].astype(jnp.bfloat16)
 
-    def terms(i, boltz, boltz_t):
-        rows = pl.ds(pl.multiple_of(i * CHUNK, CHUNK), CHUNK)
+    def terms(i, boltz, boltz_t, size):
+        rows = pl.ds(pl.multiple_of(i * size, size), size)
         denom = jnp.dot(boltz_t, weight[...], preferred_element_type=jnp.float32)
         ratio = (m_buf[rows, :].astype(jnp.float32) / denom).astype(jnp.bfloat16)
         acc[...] += jnp.dot(boltz, ratio, preferred_element_type=jnp.float32)
 
     def all_reduce(t):
-        def to_core(rows, sem):
-            return pltpu.make_async_remote_copy(
-                src_ref=acc.at[rows], dst_ref=core_recv.at[t],
-                send_sem=core_sem.at[t, 0], recv_sem=core_sem.at[t, 1],
-                device_id=device(chip, other))
-
-        core_copy = to_core(pl.ds(pl.multiple_of(other * hrows, hrows), hrows), core_sem)
-        core_copy.start()
-        core_copy.wait_recv()
-
         def part_of(at):
             return pl.ds(pl.multiple_of(at * prows, prows), prows)
 
         def row_of(core_at, chip_at):
             return pl.ds(pl.multiple_of(core_at * hrows + chip_at * prows, prows), prows)
 
-        sends = [core_copy]
-        part_copies = []
-        for d in range(1, chips):
-            to = chip_ahead(d)
+        order = list(range(chips - 1, -1, -1))
+        core_copies = {}
+        for d in order:
+            to = partner(d)
+            copy = pltpu.make_async_remote_copy(
+                src_ref=acc.at[row_of(other, to)], dst_ref=core_recv.at[t, part_of(to)],
+                send_sem=core_send.at[t, d], recv_sem=core_sem.at[t, d],
+                device_id=device(chip, other))
+            copy.start()
+            core_copies[d] = copy
+        part_copies = {}
+        for d in range(chips - 1, 0, -1):
+            to = partner(d)
+            core_copies[d].wait_recv()
             half[t, part_of(to), :] = acc[row_of(core, to), :] + core_recv[t, part_of(to), :]
             copy = pltpu.make_async_remote_copy(
                 src_ref=half.at[t, part_of(to)], dst_ref=part_recv.at[t, d - 1],
                 send_sem=part_send.at[t, d - 1], recv_sem=part_sem.at[t, d - 1],
                 device_id=device(to, core))
             copy.start()
-            part_copies.append(copy)
+            part_copies[d] = copy
+        core_copies[0].wait_recv()
         total = acc[row_of(core, chip), :] + core_recv[t, part_of(chip), :]
         for d in range(1, chips):
-            part_copies[d - 1].wait_recv()
+            part_copies[d].wait_recv()
             total = total + part_recv[t, d - 1]
         mine = row_of(core, chip)
         gathered[t, mine, :] = total
 
-        gat_copies = []
-        for d in range(1, chips):
+        gat_copies = {}
+        for d in range(chips - 1, 0, -1):
             copy = pltpu.make_async_remote_copy(
                 src_ref=gathered.at[t, mine], dst_ref=gathered.at[t, mine],
                 send_sem=gat_send.at[t, d - 1], recv_sem=gat_sem.at[t, d - 1],
-                device_id=device(chip_ahead(d), core))
-            copy.start()
-            gat_copies.append(copy)
+                device_id=device(partner(d), core))
+            copy.start()
+            gat_copies[d] = copy
         fwd_copies = []
         for d in range(chips):
             if d > 0:
-                gat_copies[d - 1].wait_recv()
-            rows = row_of(core, chip_behind(d))
+                gat_copies[d].wait_recv()
+            rows = row_of(core, partner(d))
             copy = pltpu.make_async_remote_copy(
                 src_ref=gathered.at[t, rows], dst_ref=gathered.at[t, rows],
                 send_sem=fwd_send.at[t, d], recv_sem=fwd_sem.at[t, d],
@@ -116,7 +115,7 @@
             fwd_copies.append(copy)
         for copy in fwd_copies:
             copy.wait_recv()
-        for copy in [core_copy] + part_copies + gat_copies + fwd_copies:
+        for copy in [*core_copies.values(), *part_copies.values(), *gat_copies.values(), *fwd_copies]:
             copy.wait_send()
 
     acc[...] = jnp.zeros_like(acc)
@@ -131,7 +130,7 @@
         boltz_t = boltz.T
         bzt[cols, :] = boltz_t
         m_copy(i).wait()
-        terms(i, boltz, boltz_t)
+        terms(i, boltz, boltz_t, CHUNK)
 
     pl.semaphore_wait(barrier, chips)
 
@@ -141,10 +140,10 @@
             weight[...] = (counts[...] * (gathered[t, 0:1, :] / gathered[t])).astype(jnp.bfloat16)
             acc[...] = jnp.zeros_like(acc)
 
-            @pl.loop(0, chunks)
+            @pl.loop(0, samples // BIG)
             def _(i):
-                cols = pl.ds(pl.multiple_of(i * CHUNK, CHUNK), CHUNK)
-                terms(i, bz[:, cols], bzt[cols, :])
+                cols = pl.ds(pl.multiple_of(i * BIG, BIG), BIG)
+                terms(i, bz[:, cols], bzt[cols, :], BIG)
 
     out_ref[...] = gathered[ITERS - 1]
 
@@ -180,7 +179,8 @@
             pltpu.VMEM((ITERS, states, reps), f32),
             dma((chunks,)),
             dma((chunks,)),
-            dma((ITERS, 2)),
+            dma((ITERS, chips)),
+            dma((ITERS, chips)),
             dma((ITERS, chips - 1)),
             dma((ITERS, chips - 1)),
             dma((ITERS, chips - 1)),

time: 90.8 us -> 77.8 us (0.86)
  Pallas kernels: 87.9 us -> 74.9 us
    pallas_call x1, Pallas kernels: 87.9 us -> 74.9 us  [on_device(): pl.pallas_call(functools.partial(mbar_kernel, num_dev), out_shape=jax.Sha...]
where the time goes in v2:
time: 77.8 us; the launch traced here: 77.6 us
  Pallas kernels  74.9 us (96%)
  other arithmetic  1.7 us (2%)
  local copies, waits for them, and re-layouts  0.99 us (1%)
    pallas_call x1, Pallas kernels, on_device(): pl.pallas_call(functools.partial(mbar_kernel, num_dev), out_shape=jax.Sha...  74.9 us
    sub x1, other arithmetic, on_device(): return logs[0:1] - logs  1.7 us

profile of v2, /device:TPU:0, one launch (start us, length us, event | category | flops | bytes accessed | tf_op | source)
XLA Modules:
  0.0 77.6 jit_solution(17719643262713154989)
XLA Ops:
  0.0 74.9 %shard_map.37 = f32[256,256]{1,0:T(8,128)} custom-call(s32[1,256]{1,0:T(1,128)} %bitcast.3, f32[256,12288]{1,0:T(8,128)} %e_hbm.1, s32[12288,256]{1,0:T(8,128)} %m_hbm.1), custom_call_target="tpu_custom_call" | custom-call | flops 12884901888 | bytes 25165824 | tf_op jit(solution)/shard_map/pallas_call | solution.py:159
  74.9 1.0 %log.3 = f32[256,256]{1,0:T(8,128)S(1)} log(f32[256,256]{1,0:T(8,128)} %shard_map.37) | non-fusion elementwise | bytes 524288 | tf_op jit(solution)/shard_map/log | solution.py:200
  75.9 1.7 %broadcast_subtract_fusion = f32[256,256]{1,0:T(8,128)} fusion(f32[256]{0:T(256)S(1)} %bitcast.2, f32[256,256]{1,0:T(8,128)} %shard_map.37), kind=kLoop, calls=%fused_computation | loop fusion | flops 65536 | bytes 525312 | tf_op jit(solution)/shard_map/sub | solution.py:201
  (1 shorter events, 0.0 us)
